TPU v7x, 256 devices: a whole 4x4x8 slice. The times are simulated.
256 devices in a mesh: seq: 64 (over y, z_lo, x), chan: 4 (over z_hi, core).
Axes of the slice: x: 4, y: 4, z: 8 (z_hi: 2, z_lo: 4; z = z_hi * 4 + z_lo), core: 2. Of those that a mesh axis runs over, the one named last changes fastest.
Arguments:
- tokens: bfloat16 [131072, 1, 1536], P('seq', None, 'chan'), may hold values from -24 to 24
- norm_gain_seq: bfloat16 [1536], P('chan'), may hold values from 0.099609375 to 1.8984375
- seq_left: bfloat16 [512, 256, 256], P('seq'), may hold values from -0.375 to 0.375
- seq_right: bfloat16 [256, 512, 512], P('seq'), may hold values from -0.25 to 0.25
- norm_gain_mlp: bfloat16 [1536], P('chan'), may hold values from 0.099609375 to 1.8984375
- up_first: bfloat16 [2, 4, 384, 384], P(None, 'chan'), may hold values from -0.3125 to 0.3125
- up_second: bfloat16 [2, 4, 384, 1536], P(None, 'chan'), may hold values from -0.3125 to 0.3125
- down_first: bfloat16 [4, 1536, 384], P('chan'), may hold values from -0.15625 to 0.15625
- down_second: bfloat16 [4, 384, 384], P('chan'), may hold values from -0.3125 to 0.3125
Outputs:
- layer_out: bfloat16 [131072, 1, 1536], P('seq', None, 'chan')
All inputs are finite; a program needn't handle non-finite values.
Results may differ from a plain program's by a relative error of at most 0.019.
Values may be sent and summed in bfloat16 or wider, within the bound.
A program may use at most 128 MiB of HBM per device.

v0:
```python
import jax
import jax.numpy as jnp
from jax import lax
from jax.sharding import PartitionSpec as P


def on_device(
    tokens,
    norm_gain_seq,
    seq_left,
    seq_right,
    norm_gain_mlp,
    up_first,
    up_second,
    down_first,
    down_second,
):
    local_len, doc_count, share_width = tokens.shape
    chan_count = lax.axis_size("chan")
    full_width = share_width * chan_count
    piece_width = share_width // chan_count
    tokens_float = tokens.astype(jnp.float32)
    squares = lax.psum(jnp.sum(tokens_float * tokens_float, axis=-1), "chan")
    normed = (
        tokens_float
        * lax.rsqrt(squares[..., None] / full_width + 1e-06)
        * norm_gain_seq.astype(jnp.float32)
    ).astype(jnp.bfloat16)
    blocks_here, inner_size = (seq_left.shape[0], seq_left.shape[1])
    grid_view = normed.reshape(blocks_here, inner_size, doc_count * share_width)
    first_section = jnp.einsum(
        "aob,abc->aoc", seq_left, grid_view, preferred_element_type=jnp.float32
    ).astype(jnp.bfloat16)
    second_section = jnp.einsum(
        "boa,abc->obc",
        seq_right,
        lax.all_to_all(first_section, "seq", split_axis=1, concat_axis=0, tiled=True),
        preferred_element_type=jnp.float32,
    ).astype(jnp.bfloat16)
    seq_mixed = lax.all_to_all(second_section, "seq", split_axis=0, concat_axis=1, tiled=True)
    seq_mixed = seq_mixed.reshape(local_len, doc_count, share_width)
    stream = (tokens_float + seq_mixed.astype(jnp.float32) * normed.astype(jnp.float32)).astype(
        jnp.bfloat16
    )
    stream_rows = stream.reshape(local_len * doc_count, share_width)
    row_count = stream_rows.shape[0]
    whole_rows, gain_whole = (
        lax.all_gather(stream_rows, "chan", axis=1, tiled=True),
        lax.all_gather(norm_gain_mlp, "chan", axis=0, tiled=True),
    )
    whole_float = whole_rows.astype(jnp.float32)
    mean_square = jnp.mean(whole_float * whole_float, axis=-1, keepdims=True)
    normed2 = (
        whole_float * lax.rsqrt(mean_square + 1e-06) * gain_whole.astype(jnp.float32)
    ).astype(jnp.bfloat16)
    normed2 = normed2.reshape(row_count, chan_count, share_width)
    columns = lax.all_to_all(
        up_first.reshape(2, 1, share_width, chan_count, piece_width),
        "chan",
        split_axis=3,
        concat_axis=1,
        tiled=True,
    )
    columns = columns.reshape(2, chan_count, share_width, piece_width)
    projected = jnp.einsum(
        "tij,gijq->gtiq", normed2, columns, preferred_element_type=jnp.float32
    ).astype(jnp.bfloat16)
    merged = projected.reshape(2, projected.shape[1], share_width)
    gate_up = jnp.einsum(
        "gtm,gmn->gtn", merged, up_second[:, 0], preferred_element_type=jnp.float32
    )
    hidden = (jax.nn.silu(gate_up[0]) * gate_up[1]).astype(jnp.bfloat16)
    down_rows = jnp.dot(hidden, down_first[0], preferred_element_type=jnp.float32).astype(
        jnp.bfloat16
    )
    down_rows = down_rows.reshape(down_rows.shape[0], chan_count, piece_width)
    arrived = lax.all_to_all(down_rows, "chan", split_axis=1, concat_axis=1, tiled=True)
    merged = arrived.reshape(arrived.shape[0], share_width)
    mlp_out = jnp.dot(merged, down_second[0], preferred_element_type=jnp.float32)
    layer_out = (stream_rows.astype(jnp.float32) + mlp_out).astype(jnp.bfloat16)
    return layer_out.reshape(local_len, doc_count, share_width)


def solution(mesh):
    return jax.shard_map(
        on_device,
        mesh=mesh,
        in_specs=(
            P("seq", None, "chan"),
            P("chan"),
            P("seq", None, None),
            P("seq", None, None),
            P("chan"),
            P(None, "chan", None, None),
            P(None, "chan", None, None),
            P("chan", None, None),
            P("chan", None, None),
        ),
        out_specs=P("seq", None, "chan"),
        check_vma=False,
    )
```

profile of v0, /device:TPU:71, one launch (start us, length us, event | category | flops | bytes accessed | tf_op | source)
XLA Modules:
  0.0 331.4 jit_solution(1130424778942840000)
XLA Ops:
  6.5 0.0 copy-start
  6.5 0.0 copy-start.4
  6.5 0.0 all-gather.4.cloned.1.call-start
  6.5 0.8 convert_element_type.78
  7.4 1.9 fusion.12
  9.2 9.7 %psum.7 = f32[2048,1]{0,1:T(1,128)S(1)} all-reduce(f32[2048,1]{0,1:T(1,128)S(1)} %bitcast.71), channel_id=1, replica_groups=mesh['seq'=64,'chan'=4] {'chan'}, use_global_device_ids=true, to_apply=%region_1.0 | all-reduce | flops 2048 | bytes 16384 | tf_op jit(solution)/shard_map/psum | solution.py:23
  19.0 1.8 fusion.14
  20.8 0.0 copy-done.4
  20.8 1.8 fusion.28
  22.6 2.9 copy.26
  25.6 0.0 copy-start.8
  25.6 43.7 %all_to_all.47 = bf16[8,256,384]{2,0,1:T(8,128)(2,1)S(1)} all-to-all(bf16[8,256,384]{2,0,1:T(8,128)(2,1)} %copy.26), channel_id=1, replica_groups=mesh['seq'=64,'chan'=4] {'seq'}, dimensions={1} | all-to-all | bytes 3145728 | tf_op jit(solution)/shard_map/all_to_all | solution.py:37
  69.3 0.0 copy-done.8
  69.3 2.2 fusion.29
  71.5 3.8 %copy.29 = bf16[512,4,384]{2,1,0:T(4,128)(2,1)} copy(bf16[512,4,384]{0,2,1:T(8,128)(2,1)} %fusion.29) | data formatting | bytes 3145728 | tf_op jit(solution)/shard_map/convert_element_type | solution.py:39
  75.3 44.9 %all_to_all.48 = bf16[512,4,384]{2,1,0:T(4,128)(2,1)S(1)} all-to-all(bf16[512,4,384]{2,1,0:T(4,128)(2,1)} %copy.29), channel_id=1, replica_groups=mesh['seq'=64,'chan'=4] {'seq'}, dimensions={0} | all-to-all | bytes 3145728 | tf_op jit(solution)/shard_map/all_to_all | solution.py:40
  120.2 0.2 convert_bitcast_fusion
  120.5 3.7 %copy.31 = f32[8,64,4,384]{3,2,1,0:T(4,128)} copy(f32[8,64,4,384]{3,0,1,2:T(8,128)S(1)} %convert_bitcast_fusion) | data formatting | bytes 6291456 | tf_op jit(solution)/shard_map/convert_element_type | solution.py:42
  124.1 5.0 %reshape.87 = f32[2048,1,384]{2,0,1:T(8,128)} reshape(f32[8,64,4,384]{3,2,1,0:T(4,128)} %copy.31) | data formatting | bytes 6291456 | tf_op jit(solution)/shard_map/convert_element_type | solution.py:42
  129.1 4.2 %fusion.15 = bf16[2048,1,384]{2,0,1:T(8,128)(2,1)} fusion(bf16[2048,1,384]{2,0,1:T(8,128)(2,1)} %param.9, f32[2048,1,384]{2,0,1:T(8,128)} %reshape.87, f32[384]{0:T(512)S(1)} %convert_element_type.78, f32[2048]{0:T(1024)S(1)} %bitcast.70), kind=kLoop, calls=%fused_computation.18 | loop fusion | flops 6291456 | bytes 6301184 | tf_op jit(solution)/shard_map/convert_element_type | solution.py:42
  133.3 0.0 all-gather.4.cloned.1.call-update
  133.3 0.0 copy-done.5
  133.4 0.3 copy.32
  133.7 0.9 copy.33
  134.6 8.5 %all-to-all-start.2 = ((bf16[2,1,384,4,96]{2,4,0,1,3:T(8,128)(2,1)}), bf16[2,1,384,4,96]{2,4,0,1,3:T(8,128)(2,1)S(1)}, u32[]{:S(2)}, u32[]{:S(2)}) async-start(bf16[2,1,384,4,96]{2,4,0,1,3:T(8,128)(2,1)} %copy.33), calls=%async_computation.2 | async-start | bytes 1179648 | tf_op jit(solution)/shard_map/all_to_all | solution.py:57
  143.1 0.0 copy-done.7
  143.1 33.9 %all-gather.1 = bf16[4,1,384]{2,1,0:T(2,128)(2,1)S(1)} all-gather(bf16[1,1,384]{2,1,0:T(2,128)(2,1)S(1)} %reshape.92), channel_id=1, replica_groups=mesh['seq'=64,'chan'=4] {'chan'}, dimensions={0}, use_global_device_ids=true | all-gather | bytes 3840 | tf_op jit(solution)/shard_map/all_gather | solution.py:49
  177.0 54.5 %all-gather.4.cloned.1.call-done = bf16[2048,1,1536]{2,0,1:T(8,128)(2,1)} async-done(((bf16[2048,1,384]{2,0,1:T(8,128)(2,1)}), bf16[2048,1,1536]{2,0,1:T(8,128)(2,1)}) %all-gather.4.cloned.1.call-update) | async-done | bytes 6291472 | tf_op jit(solution)/shard_map/all_gather | solution.py:48
  231.6 4.2 %fusion = f32[2048]{0:T(1024)S(1)} fusion(bf16[2048,1,1536]{2,0,1:T(8,128)(2,1)} %all-gather.4.cloned.1.call-done), kind=kLoop, calls=%fused_computation.2 | loop fusion | flops 9435136 | bytes 6299648 | tf_op jit(solution)/shard_map/reduce_sum | solution.py:52
  235.8 0.4 copy-done.2
  236.2 4.1 %fusion.2 = bf16[2048,1536]{1,0:T(8,128)(2,1)} fusion(bf16[2048,1,1536]{2,0,1:T(8,128)(2,1)S(1)} %copy-done.2, f32[1536]{0:T(1024)S(1)} %reshape.94, f32[2048]{0:T(1024)S(1)} %add_rsqrt_fusion), kind=kLoop, calls=%fused_computation.4 | loop fusion | flops 12582912 | bytes 12597248 | tf_op jit(solution)/shard_map/convert_element_type | solution.py:55
  240.3 11.3 %reshape.80 = bf16[2048,4,384]{2,1,0:T(4,128)(2,1)} reshape(bf16[2048,1536]{1,0:T(8,128)(2,1)} %fusion.2) | data formatting | bytes 12582912 | tf_op jit(solution)/shard_map/reshape | solution.py:56
  251.6 0.0 all-to-all-done.2
  251.6 5.2 %fusion.17 = bf16[2,2048,4,96]{1,3,0,2:T(8,128)(2,1)S(1)} fusion(bf16[2048,4,384,1]{2,1,0,3:T(4,128)(2,1)} %bitcast.63, bf16[2,1,384,4,96]{2,4,0,1,3:T(8,128)(2,1)S(1)} %all-to-all-done.2), kind=kOutput, calls=%fused_computation.22 | convolution fusion | flops 1209532416 | bytes 10027008 | tf_op jit(solution)/shard_map/tij,gijq->gtiq/dot_general | solution.py:65
  256.8 0.4 copy.35
  257.3 0.0 copy-done
  257.3 0.0 copy-start.9
  257.3 11.7 %fusion.24 = f32[2,2048,1536]{2,1,0:T(8,128)} fusion(bf16[2,2048,384]{1,2,0:T(8,128)(2,1)S(1)} %bitcast.62, bf16[2,1,384,1536]{3,2,1,0:T(8,128)(2,1)S(1)} %copy-done), kind=kOutput, calls=%fused_computation.25 | convolution fusion | flops 4831838208 | bytes 30670848 | tf_op jit(solution)/shard_map/gtm,gmn->gtn/dot_general | solution.py:69
  269.0 0.0 copy-done.9
  269.0 10.6 %fusion.20 = bf16[2048,384]{0,1:T(8,128)(2,1)S(1)} fusion(f32[2,2048,1536]{2,1,0:T(8,128)} %fusion.24, bf16[1,1536,384]{2,1,0:T(8,128)(2,1)S(1)} %copy-done.9), kind=kOutput, calls=%fused_computation.23 | convolution fusion | flops 2435579904 | bytes 27918336 | tf_op jit(solution)/shard_map/dot_general | solution.py:73
  279.6 0.0 copy-start.3
  279.6 0.0 copy-start.6
  279.7 0.0 copy-start.1
  279.7 42.5 %all_to_all.49 = bf16[2048,4,96]{0,2,1:T(8,128)(2,1)S(1)} all-to-all(bf16[2048,4,96]{0,2,1:T(8,128)(2,1)S(1)} %bitcast.68), channel_id=1, replica_groups=mesh['seq'=64,'chan'=4] {'chan'}, dimensions={1} | all-to-all | bytes 3145728 | tf_op jit(solution)/shard_map/all_to_all | solution.py:77
  322.2 0.0 copy-done.3
  322.2 0.0 copy-done.6
  322.2 2.3 fusion.23
  324.6 0.0 copy-done.1
  (8 shorter events, 0.1 us)
Async XLA Ops:
  6.5 250.7 %copy-start = (bf16[2,1,384,1536]{3,2,1,0:T(8,128)(2,1)S(1)}, bf16[2,1,384,1536]{3,2,1,0:T(8,128)(2,1)}, u32[]{:S(2)}) copy-start(bf16[2,1,384,1536]{3,2,1,0:T(8,128)(2,1)} %param.15) | copy-start | bytes 7077892
  6.5 14.3 %copy-start.4 = (bf16[8,256,256]{2,1,0:T(8,128)(2,1)S(1)}, bf16[8,256,256]{2,1,0:T(8,128)(2,1)}, u32[]{:S(2)}) copy-start(bf16[8,256,256]{2,1,0:T(8,128)(2,1)} %param.11) | copy-start | bytes 3145732
  6.5 225.0 %all-gather.4.cloned.1.call-start = ((), (), s32[]{:S(2)}) async-start(), calls=%async_computation.4 | async-start | bytes 7864320 | tf_op jit(solution)/shard_map/all_gather | solution.py:48
  25.6 43.7 %copy-start.8 = (bf16[4,512,512]{2,1,0:T(8,128)(2,1)S(1)}, bf16[4,512,512]{2,1,0:T(8,128)(2,1)}, u32[]{:S(2)}) copy-start(bf16[4,512,512]{2,1,0:T(8,128)(2,1)} %param.12) | copy-start | bytes 6291460
  129.1 4.3 %copy-start.5 = (bf16[2,1,384,384]{3,2,1,0:T(8,128)(2,1)S(1)}, bf16[2,1,384,384]{3,2,1,0:T(8,128)(2,1)}, u32[]{:S(2)}) copy-start(bf16[2,1,384,384]{3,2,1,0:T(8,128)(2,1)} %param.14) | copy-start | bytes 1769476
  133.3 9.8 %copy-start.7 = (bf16[384]{0:T(512)(128)(2,1)S(1)}, bf16[384]{0:T(512)(128)(2,1)}, u32[]{:S(2)}) copy-start(bf16[384]{0:T(512)(128)(2,1)} %param.13) | copy-start | bytes 2308
  134.6 117.0 %all-to-all-start.2 = ((bf16[2,1,384,4,96]{2,4,0,1,3:T(8,128)(2,1)}), bf16[2,1,384,4,96]{2,4,0,1,3:T(8,128)(2,1)S(1)}, u32[]{:S(2)}, u32[]{:S(2)}) async-start(bf16[2,1,384,4,96]{2,4,0,1,3:T(8,128)(2,1)} %copy.33), calls=%async_computation.2 | async-start | bytes 1179648 | tf_op jit(solution)/shard_map/all_to_all | solution.py:57
  231.6 4.6 %copy-start.2 = (bf16[2048,1,1536]{2,0,1:T(8,128)(2,1)S(1)}, bf16[2048,1,1536]{2,0,1:T(8,128)(2,1)}, u32[]{:S(2)}) copy-start(bf16[2048,1,1536]{2,0,1:T(8,128)(2,1)} %all-gather.4.cloned.1.call-done) | copy-start | bytes 18874372
  257.3 11.7 %copy-start.9 = (bf16[1,1536,384]{2,1,0:T(8,128)(2,1)S(1)}, bf16[1,1536,384]{2,1,0:T(8,128)(2,1)}, u32[]{:S(2)}) copy-start(bf16[1,1536,384]{2,1,0:T(8,128)(2,1)} %param.16) | copy-start | bytes 3538948
  279.6 42.6 %copy-start.3 = (bf16[2048,1,384]{2,0,1:T(8,128)(2,1)S(1)}, bf16[2048,1,384]{2,0,1:T(8,128)(2,1)}, u32[]{:S(2)}) copy-start(bf16[2048,1,384]{2,0,1:T(8,128)(2,1)} %fusion.15) | copy-start | bytes 4718596
  279.6 42.6 %copy-start.6 = (bf16[1,384,384]{2,1,0:T(8,128)(2,1)S(1)}, bf16[1,384,384]{2,1,0:T(8,128)(2,1)}, u32[]{:S(2)}) copy-start(bf16[1,384,384]{2,1,0:T(8,128)(2,1)} %param.17) | copy-start | bytes 884740
  279.7 44.9 %copy-start.1 = (bf16[2,1,384,1536]{3,2,1,0:T(8,128)(2,1)S(1)}, bf16[2,1,384,1536]{3,2,1,0:T(8,128)(2,1)}, u32[]{:S(2)}) copy-start(bf16[2,1,384,1536]{3,2,1,0:T(8,128)(2,1)} %param.15) | copy-start | bytes 7077892
Sparse Core Ops, SparseCore 0:
  133.5 98.0 all-gather.3
where the time goes:
time: 337 us; the launch traced here: 331 us
  blocking collectives  175 us (52%)
  waiting for transfers between devices  54.5 us (16%)
  matrix products  34 us (10%)
  local copies, waits for them, and re-layouts  28.7 us (9%)
  other arithmetic  17.4 us (5%)
  between operations  13.5 us (4%)
  starting transfers between devices  8.54 us (3%)
    all_gather x1, waiting for transfers between devices, on_device(): lax.all_gather(stream_rows, 'chan', axis=1, tiled=True)  54.5 us
    all_to_all x1, blocking collectives, on_device(): lax.all_to_all(second_section, 'seq', split_axis=0, concat_axis=1, tiled=...  44.9 us
    all_to_all x1, blocking collectives, on_device(): lax.all_to_all(first_section, 'seq', split_axis=1, concat_axis=0, tiled=T...  43.7 us
    all_to_all x1, blocking collectives, on_device(): lax.all_to_all(down_rows, 'chan', split_axis=1, concat_axis=1, tiled=True)  42.5 us
    all_gather x1, blocking collectives, on_device(): lax.all_gather(norm_gain_mlp, 'chan', axis=0, tiled=True)  33.9 us
    dot_general x1, matrix products, on_device(): jnp.einsum('gtm,gmn->gtn', merged, up_second[:, 0], preferred_element_typ...  11.7 us
    reshape x1, local copies, waits for them, and re-layouts, on_device(): normed2 = normed2.reshape(row_count, chan_count, share_width)  11.3 us
    dot_general x1, matrix products, on_device(): jnp.dot(hidden, down_first[0], preferred_element_type=jnp.float32)  10.6 us
  transfers between devices with their start and end apart: 2, of which 1 were waited for; matrix products, arithmetic and copies ran while one was open for 6% of the time, Pallas kernels for 0%

commit v1 on v0

v1 whole, which is shorter than its diff:
```python
import jax
import jax.numpy as jnp
from jax import lax
from jax.experimental import pallas as pl
from jax.experimental.pallas import tpu as pltpu
from jax.sharding import PartitionSpec as P

MESH = pl.DeviceIdType.MESH
BF16 = jnp.bfloat16
F32 = jnp.float32
W = 384
EPS = 1e-6


def dot(a, b):
    return jnp.dot(a, b, preferred_element_type=F32)


def remote(src, dst, send, recv, device):
    return pltpu.make_async_remote_copy(
        src_ref=src, dst_ref=dst, send_sem=send, recv_sem=recv, device_id=device, device_id_type=MESH
    )


def drain(ref, sem):
    pltpu.make_async_copy(ref, ref, sem).wait()


def layer_kernel(
    tok_in, gains_in, left_in, right_in, upf_in, ups_in, dnf_in, dns_in,
    out,
    X, GS, GM, SL, SR, SQ, RR, RC, FS, S1, R1, GB, S2, R2, ST, TS, OB, UF, US, DF, DS,
    ld, sq_sem, gm_sem, a1_sem, a2_sem, st_sem, out_send, out_recv, w1_send, w1_recv, wr_send, wr_recv, sib_send, sib_recv,
):
    s = lax.axis_index("seq")
    ch = lax.axis_index("chan")
    y, l, x = s // 16, (s // 4) % 4, s % 4
    sib = ch + 1 - 2 * (ch % 2)
    opp = (ch + 2) % 4

    def seq_of(yy, ll, xx):
        return yy * 16 + ll * 4 + xx

    mirror = (seq_of(y, 3 - l, x), opp)
    x_plus, x_minus = (seq_of(y, l, (x + 1) % 4), ch), (seq_of(y, l, (x + 3) % 4), ch)
    y_plus, y_minus = (seq_of((y + 1) % 4, l, x), ch), (seq_of((y + 3) % 4, l, x), ch)

    bar = pltpu.get_barrier_semaphore()

    @pl.loop(1, 64)
    def _(k):
        pl.semaphore_signal(bar, inc=1, device_id=((s + k) % 64, ch), device_id_type=MESH)

    @pl.loop(1, 4)
    def _(k):
        pl.semaphore_signal(bar, inc=1, device_id=(s, (ch + k) % 4), device_id_type=MESH)

    pl.semaphore_signal(bar, inc=1, device_id=mirror, device_id_type=MESH)

    loads = [
        pltpu.make_async_copy(tok_in, X, ld.at[0]),
        pltpu.make_async_copy(gains_in.at[0], GS, ld.at[1]),
        pltpu.make_async_copy(gains_in.at[1], GM.at[ch], ld.at[2]),
        pltpu.make_async_copy(left_in, SL, ld.at[3]),
        pltpu.make_async_copy(right_in, SR, ld.at[4]),
        pltpu.make_async_copy(ups_in, US.at[ch, :, pl.ds(0, 96)], ld.at[5]),
        pltpu.make_async_copy(upf_in, UF.at[ch], ld.at[6]),
        pltpu.make_async_copy(dnf_in, DF.at[ch], ld.at[7]),
        pltpu.make_async_copy(dns_in, DS.at[ch, :, pl.ds(0, 96)], ld.at[8]),
    ]
    for c in loads:
        c.start()

    eye = lax.broadcasted_iota(jnp.int32, (128, 128), 0) == lax.broadcasted_iota(jnp.int32, (128, 128), 1)
    loads[0].wait()

    @pl.loop(0, 16)
    def _(k):
        xb = X[pl.ds(pl.multiple_of(k * 128, 128), 128), :].astype(F32)
        col = jnp.sum(xb * xb, axis=1, keepdims=True)
        SQ[ch, pl.ds(k, 1), :] = jnp.sum(jnp.where(eye, col, 0.0), axis=0, keepdims=True)

    loads[2].wait()
    pl.semaphore_wait(bar, 67)

    @pl.loop(1, 4)
    def _(k):
        to = (s, (ch + k) % 4)
        remote(SQ.at[ch], SQ.at[ch], sq_sem.at[0], sq_sem.at[1], to).start()
        remote(GM.at[ch], GM.at[ch], gm_sem.at[0], gm_sem.at[1], to).start()

    ux = y * 4 + x
    uy = x * 4 + y

    def us_unit(blk, u, lanes=pl.ds(0, 1536)):
        return US.at[blk, u // 2, pl.ds(pl.multiple_of((u % 2) * 48, 16), 48), lanes]

    def us_row(blk, r, lanes=pl.ds(0, 1536)):
        return US.at[blk, pl.ds(r * 2, 2), pl.ds(0, 96), lanes]

    def uf_unit(blk, u, lanes=pl.ds(0, 512)):
        return UF.at[blk, pl.ds(pl.multiple_of(u * 48, 16), 48), lanes]

    def uf_row(blk, r, lanes=pl.ds(0, 512)):
        return UF.at[blk, pl.ds(pl.multiple_of(r * 192, 16), 192), lanes]

    def df_unit(blk, u, lanes=pl.ds(0, 512)):
        return DF.at[blk, pl.ds(pl.multiple_of(u * 96, 16), 96), lanes]

    def df_row(blk, r, lanes=pl.ds(0, 512)):
        return DF.at[blk, pl.ds(pl.multiple_of(r * 384, 16), 384), lanes]

    first_unit = [
        remote(ups_in.at[ux // 2, pl.ds(pl.multiple_of((ux % 2) * 48, 16), 48)], us_unit(ch, ux), w1_send.at[0], w1_recv.at[0], mirror),
        remote(upf_in.at[pl.ds(pl.multiple_of(uy * 48, 16), 48)], uf_unit(ch, uy), w1_send.at[1], w1_recv.at[1], mirror),
        remote(dnf_in.at[pl.ds(pl.multiple_of(uy * 96, 16), 96)], df_unit(ch, uy), w1_send.at[2], w1_recv.at[2], mirror),
        remote(dns_in, DS.at[ch, :, pl.ds(0, 96)], w1_send.at[3], w1_recv.at[3], mirror),
    ]
    for c in first_unit:
        c.start()

    to_sib = (s, sib)
    own_block = [
        remote(ups_in, US.at[ch, :, pl.ds(0, 96)], sib_send.at[0], sib_recv.at[0], to_sib),
        remote(upf_in, UF.at[ch], sib_send.at[1], sib_recv.at[1], to_sib),
        remote(dnf_in, DF.at[ch], sib_send.at[2], sib_recv.at[2], to_sib),
        remote(dns_in, DS.at[ch, :, pl.ds(0, 96)], sib_send.at[3], sib_recv.at[3], to_sib),
    ]
    other_block = [
        remote(US.at[opp, :, pl.ds(0, 96)], US.at[opp, :, pl.ds(0, 96)], sib_send.at[4], sib_recv.at[4], to_sib),
        remote(UF.at[opp], UF.at[opp], sib_send.at[5], sib_recv.at[5], to_sib),
        remote(DF.at[opp], DF.at[opp], sib_send.at[6], sib_recv.at[6], to_sib),
        remote(DS.at[opp, :, pl.ds(0, 96)], DS.at[opp, :, pl.ds(0, 96)], sib_send.at[7], sib_recv.at[7], to_sib),
    ]
    for c in own_block:
        c.start()

    xring, yring = (x, x_plus, x_minus), (y, y_plus, y_minus)
    ux_of = (lambda p: y * 4 + p, lambda p: p)
    uy_of = (lambda p: x * 4 + p, lambda p: p)
    tables = [
        (us_unit, us_row, 768, xring, yring, ux_of),
        (uf_unit, uf_row, 256, yring, xring, uy_of),
        (df_unit, df_row, 256, yring, xring, uy_of),
    ]

    def ring_copies(stage, step):
        copies = []
        for j, (unit, row, half, ring_a, ring_b, (first, second)) in enumerate(tables):
            pos, plus, minus = (ring_a, ring_b)[stage]
            part, index = ((unit, first), (row, second))[stage]
            sem = ((j * 2 + stage) * 2 + step) * 2
            if step == 0:
                mine = part(opp, index(pos))
                copies += [
                    remote(mine, mine, wr_send.at[sem], wr_recv.at[sem], plus),
                    remote(mine, mine, wr_send.at[sem + 1], wr_recv.at[sem + 1], minus),
                ]
            else:
                below = part(opp, index((pos + 3) % 4), pl.ds(0, half))
                above = part(opp, index((pos + 1) % 4), pl.ds(half, half))
                copies += [
                    remote(below, below, wr_send.at[sem], wr_recv.at[sem], plus),
                    remote(above, above, wr_send.at[sem + 1], wr_recv.at[sem + 1], minus),
                ]
        return copies

    rings = [ring_copies(0, 0), ring_copies(0, 1), ring_copies(1, 0), ring_copies(1, 1)]

    US[:, :, pl.ds(96, 32), :] = jnp.zeros((4, 8, 32, 1536), BF16)
    DS[:, :, pl.ds(96, 32), :] = jnp.zeros((4, 4, 32, W), BF16)

    drain(SQ.at[pl.ds(0, 3)], sq_sem.at[1])
    scale = lax.rsqrt((SQ[0] + SQ[1] + SQ[2] + SQ[3]) / 1536.0 + EPS)
    RR[...] = scale
    for c in (loads[1], loads[3]):
        c.wait()
    gain = GS[pl.ds(0, 1), :].astype(F32)

    @pl.loop(0, 8)
    def _(o):
        r = jnp.concatenate([RR[pl.ds(2 * o, 1), :], RR[pl.ds(2 * o + 1, 1), :]], axis=1)
        lw = (SL[o].astype(F32) * r).astype(BF16)
        rows = X[pl.ds(pl.multiple_of(o * 256, 256), 256), :]
        FS[o] = (dot(lw, rows) * gain).astype(BF16)

    out_row = lax.broadcasted_iota(jnp.int32, (256, 256), 0)
    in_row = lax.broadcasted_iota(jnp.int32, (256, 256), 1)
    perm = (in_row == (out_row & 7) * 32 + (out_row >> 5) * 4 + ((out_row >> 3) & 3)).astype(F32).astype(BF16)
    back = (out_row == (in_row & 7) * 32 + (in_row >> 5) * 4 + ((in_row >> 3) & 3)).astype(F32).astype(BF16)

    def a2a_send(src, dst, sems, d):
        @pl.when(d != s)
        def _():
            remote(src.at[d], dst.at[s], sems.at[0], sems.at[1], (d, ch)).start()

    @pl.loop(0, 8)
    def _(k):
        g = (k + s // 8) % 8
        block = FS[:, pl.ds(pl.multiple_of(g * 32, 32), 32), :].reshape(256, W)
        S1[pl.ds(g * 8, 8)] = dot(perm, block).astype(BF16).reshape(8, 32, W)

        @pl.loop(0, 8)
        def _(j):
            a2a_send(S1, R1, a1_sem, g * 8 + (j + s) % 8)

    R1[s] = S1[s]
    for c in first_unit:
        c.wait_recv()
    for c in rings[0]:
        c.start()

    @pl.loop(0, 16)
    def _(k):
        col = jnp.sum(jnp.where(eye, RR[pl.ds(k, 1), :], 0.0), axis=1, keepdims=True)
        RC[pl.ds(pl.multiple_of(k * 128, 128), 128), :] = jnp.broadcast_to(col, (128, 128))

    loads[4].wait()
    drain(R1.at[pl.ds(0, 63)], a1_sem.at[1])
    for c in rings[0]:
        c.wait_recv()
    for c in rings[1]:
        c.start()

    @pl.loop(0, 8)
    def _(g):
        part = R1[pl.ds(g * 8, 8)].astype(F32)
        for b in range(4):
            rows = part[:, 8 * b : 8 * b + 8, :].reshape(64, W)
            GB[b, pl.ds(pl.multiple_of(g * 64, 64), 64), :] = rows.astype(BF16)

    @pl.loop(0, 2)
    def _(k):
        m = (k + s // 32) % 2
        for pair in range(2):
            halves = [
                dot(SR[b, pl.ds(pl.multiple_of(m * 256, 256), 256), :], GB[b]).reshape(32, 8, W)
                for b in (2 * pair, 2 * pair + 1)
            ]
            S2[pl.ds(m * 32, 32), pl.ds(16 * pair, 16), :] = jnp.concatenate(halves, axis=1).astype(BF16)

        @pl.loop(0, 32)
        def _(j):
            a2a_send(S2, R2, a2_sem, m * 32 + (j + s) % 32)

    R2[s] = S2[s]
    for c in rings[1]:
        c.wait_recv()
    for c in rings[2]:
        c.start()
    drain(R2.at[pl.ds(0, 63)], a2_sem.at[1])

    @pl.loop(0, 8)
    def _(g):
        mixed = dot(back, R2[pl.ds(g * 8, 8)].reshape(256, W)).reshape(8, 32, W)
        for o in range(8):
            at = pl.ds(pl.multiple_of(o * 256 + g * 32, 32), 32)
            rc = RC[at, :]
            xs = X[at, :].astype(F32)
            normed = (xs * jnp.concatenate([rc, rc, rc], axis=1) * gain).astype(BF16).astype(F32)
            ST[at, :] = (xs + mixed[o] * normed).astype(BF16)

    @pl.loop(1, 4)
    def _(k):
        q = (ch + k) % 4
        remote(ST.at[pl.ds(pl.multiple_of(q * 512, 512), 512)], TS.at[ch], st_sem.at[0], st_sem.at[1], (s, q)).start()

    TS[ch] = ST[pl.ds(pl.multiple_of(ch * 512, 512), 512), :]
    for c in rings[2]:
        c.wait_recv()
    for c in rings[3]:
        c.start()
    for c in rings[3]:
        c.wait_recv()
    for c in other_block:
        c.start()
    for c in loads[5:]:
        c.wait()
    drain(GM.at[pl.ds(0, 3)], gm_sem.at[1])
    for c in own_block:
        c.wait_recv()
    drain(TS.at[pl.ds(0, 3)], st_sem.at[1])
    for c in other_block:
        c.wait_recv()

    @pl.loop(0, 2)
    def _(t):
        at = pl.ds(pl.multiple_of(t * 256, 256), 256)
        squares = jnp.zeros((256, 1), F32)
        for i in range(4):
            v = TS[i, at, :].astype(F32)
            squares += jnp.sum(v * v, axis=1, keepdims=True)
        r2 = lax.rsqrt(squares / 1536.0 + EPS)
        projected = []
        for i in range(4):
            n = (TS[i, at, :].astype(F32) * r2 * GM[i, pl.ds(0, 1), :].astype(F32)).astype(BF16)
            projected.append([dot(n, UF[i, pl.ds(g * W, W), :]).astype(BF16) for g in range(2)])
        down = []
        for p in range(4):
            merged = [
                jnp.concatenate([projected[i][g][:, p * 128 : p * 128 + 128] for i in range(4)], axis=1) for g in range(2)
            ]
            acc = jnp.zeros((256, 512), F32)
            for n in range(3):
                lanes = pl.ds(n * 512, 512)
                gate, up = (dot(merged[g], US[p, pl.ds(g * 4, 4), :, lanes].reshape(512, 512)) for g in range(2))
                hidden = (gate / (1.0 + jnp.exp(-gate)) * up).astype(BF16)
                acc += dot(hidden, DF[p, pl.ds(n * 512, 512), :])
            down.append(acc.astype(BF16))
        for r in range(4):
            merged = jnp.concatenate([down[p][:, r * 128 : r * 128 + 128] for p in range(4)], axis=1)
            mlp = dot(merged, DS[r].reshape(512, W))
            OB[r, at, :] = (TS[r, at, :].astype(F32) + mlp).astype(BF16)
        home = pl.ds(pl.multiple_of(ch * 512 + t * 256, 256), 256)
        out[home, :] = OB[ch, at, :]

        @pl.loop(1, 4)
        def _(k):
            r = (ch + k) % 4
            remote(OB.at[r, at], out.at[home], out_send.at[t], out_recv.at[t], (s, r)).start()

    drain(SQ.at[pl.ds(0, 3)], sq_sem.at[0])
    drain(GM.at[pl.ds(0, 3)], gm_sem.at[0])
    drain(S1.at[pl.ds(0, 63)], a1_sem.at[0])
    drain(S2.at[pl.ds(0, 63)], a2_sem.at[0])
    drain(TS.at[pl.ds(0, 3)], st_sem.at[0])
    for c in first_unit + own_block + other_block + rings[0] + rings[1] + rings[2] + rings[3]:
        c.wait_send()
    for t in range(2):
        drain(out.at[pl.ds(0, 768)], out_send.at[t])
        drain(out.at[pl.ds(0, 768)], out_recv.at[t])


def on_device(
    tokens, norm_gain_seq, seq_left, seq_right, norm_gain_mlp, up_first, up_second, down_first, down_second
):
    rows = tokens.shape[0]
    gains = jnp.broadcast_to(jnp.stack([norm_gain_seq, norm_gain_mlp])[:, None, :], (2, 16, W))
    upf = jnp.pad(up_first.reshape(768, 4, 96), ((0, 0), (0, 0), (0, 32))).reshape(768, 512)
    dnf = jnp.pad(down_first.reshape(1536, 4, 96), ((0, 0), (0, 0), (0, 32))).reshape(1536, 512)
    hbm = pl.BlockSpec(memory_space=pl.ANY)
    dma = pltpu.SemaphoreType.DMA
    out = pl.pallas_call(
        layer_kernel,
        out_shape=jax.ShapeDtypeStruct((rows, W), BF16),
        in_specs=[hbm] * 8,
        out_specs=pl.BlockSpec(memory_space=pltpu.VMEM),
        scratch_shapes=[
            pltpu.VMEM((2048, W), BF16),
            pltpu.VMEM((16, W), BF16),
            pltpu.VMEM((4, 16, W), BF16),
            pltpu.VMEM((8, 256, 256), BF16),
            pltpu.VMEM((4, 512, 512), BF16),
            pltpu.VMEM((4, 16, 128), F32),
            pltpu.VMEM((16, 128), F32),
            pltpu.VMEM((2048, 128), F32),
            pltpu.VMEM((8, 256, W), BF16),
            pltpu.VMEM((64, 32, W), BF16),
            pltpu.VMEM((64, 32, W), BF16),
            pltpu.VMEM((4, 512, W), BF16),
            pltpu.VMEM((64, 32, W), BF16),
            pltpu.VMEM((64, 32, W), BF16),
            pltpu.VMEM((2048, W), BF16),
            pltpu.VMEM((4, 512, W), BF16),
            pltpu.VMEM((4, 512, W), BF16),
            pltpu.VMEM((4, 768, 512), BF16),
            pltpu.VMEM((4, 8, 128, 1536), BF16),
            pltpu.VMEM((4, 1536, 512), BF16),
            pltpu.VMEM((4, 4, 128, W), BF16),
            dma((9,)), dma((2,)), dma((2,)), dma((2,)), dma((2,)), dma((2,)), dma((2,)), dma((2,)),
            dma((4,)), dma((4,)), dma((24,)), dma((24,)), dma((8,)), dma((8,)),
        ],
        compiler_params=pltpu.CompilerParams(
            collective_id=0, has_side_effects=True, vmem_limit_bytes=60 * 2**20
        ),
        name="layer",
    )(
        tokens.reshape(rows, W), gains, seq_left, seq_right, upf,
        up_second.reshape(8, 96, 1536), dnf, down_second.reshape(4, 96, W),
    )
    return out.reshape(rows, 1, W)


def solution(mesh):
    return jax.shard_map(
        on_device,
        mesh=mesh,
        in_specs=(
            P("seq", None, "chan"),
            P("chan"),
            P("seq", None, None),
            P("seq", None, None),
            P("chan"),
            P(None, "chan", None, None),
            P(None, "chan", None, None),
            P("chan", None, None),
            P("chan", None, None),
        ),
        out_specs=P("seq", None, "chan"),
        check_vma=False,
    )
```

time: 337 us -> 182 us (0.54)
  the two profiles are of different devices: /device:TPU:71 before, /device:TPU:39 now
where the time goes in v1:
time: 182 us
  Pallas kernels  170 us (93%)
  local copies, waits for them, and re-layouts  11.8 us (6%)
    pallas_call x1, Pallas kernels, on_device(): pl.pallas_call(layer_kernel, out_shape=jax.ShapeDtypeStruct((rows, W), BF...  170 us
    unnamed x3, local copies, waits for them, and re-layouts  6.52 us

profile of v1, /device:TPU:39, one launch (start us, length us, event | category | flops | bytes accessed | tf_op | source)
XLA Modules:
  0.0 181.6 jit_solution(3601193356180141037)
XLA Ops:
  0.0 0.7 stack.9
  0.7 0.7 stack.10
  1.4 0.6 broadcast_in_dim.2.gains_in
  2.0 2.2 %copy.10 = bf16[2,1,384,384]{2,0,3,1:T(2,128)(2,1)S(1)} copy(bf16[2,1,384,384]{3,2,1,0:T(8,128)(2,1)} %param.14) | data formatting | bytes 1179648 | tf_op args[5]
  4.2 0.4 reshape.26
  4.6 0.1 pad.8
  4.7 1.2 copy.14.upf_in
  5.8 1.6 copy.12
  7.4 0.1 pad.9
  7.5 1.6 copy.15.dnf_in
  9.1 169.8 %layer.1 = bf16[2048,384]{1,0:T(8,128)(2,1)} custom-call(bf16[2048,384]{1,0:T(8,128)(2,1)} %bitcast.14, bf16[2,16,384]{2,1,0:T(8,128)(2,1)} %broadcast_in_dim.2.gains_in, bf16[8,256,256]{2,1,0:T(8,128)(2,1)} %left_in.1, bf16[4,512,512]{2,1,0:T(8,128)(2,1)} %right_in.1, bf16[768,512]{1,0:T(8,128)(2,1)} %copy.14.upf_in, bf16[8,96,1536]{2,1,0:T(8,128)(2,1)} %bitcast.13, ...), custom_call_target="tpu_custom_call" | custom-call | tf_op jit(solution)/shard_map/layer/pallas_call | solution.py:343
  178.9 2.7 %copy.17 = bf16[2048,1,384]{2,0,1:T(8,128)(2,1)} copy(bf16[2048,1,384]{2,0,1:T(8,128)(2,1)} %bitcast.9) | data formatting | bytes 3145728
  (1 shorter events, 0.0 us)

commit v2 on v1

v2 whole, which is shorter than its diff:
```python
import jax
import jax.numpy as jnp
from jax import lax
from jax.experimental import pallas as pl
from jax.experimental.pallas import tpu as pltpu
from jax.sharding import PartitionSpec as P

MESH = pl.DeviceIdType.MESH
BF16 = jnp.bfloat16
F32 = jnp.float32
W = 384
EPS = 1e-6


def dot(a, b):
    return jnp.dot(a, b, preferred_element_type=F32)


def remote(src, dst, send, recv, device):
    return pltpu.make_async_remote_copy(
        src_ref=src, dst_ref=dst, send_sem=send, recv_sem=recv, device_id=device, device_id_type=MESH
    )


def drain(ref, sem):
    pltpu.make_async_copy(ref, ref, sem).wait()


def layer_kernel(
    tok_in, gseq_in, gmlp_in, left_in, right_in, upf_in, ups_in, dnf_in, dns_in,
    out,
    X, G, SL, SR, SQ, RR, RC, FS, S1, R1, GB, S2, R2, MB, XB, ST, TS, OB, UF, US, DF, DS, UR, DR,
    ld, sq_sem, gm_sem, xb_sem, a1_sem, a2_sem, mb_sem, st_sem, out_send, out_recv, w1_send, w1_recv, wr_send, wr_recv, sib_send, sib_recv,
):
    s = lax.axis_index("seq")
    ch = lax.axis_index("chan")
    y, l, x = s // 16, (s // 4) % 4, s % 4
    sib = ch + 1 - 2 * (ch % 2)
    opp = (ch + 2) % 4
    h, c = ch // 2, ch % 2
    side = l // 2
    far = 2 * (1 - h)

    def seq_of(yy, ll, xx):
        return yy * 16 + ll * 4 + xx

    mirror = (seq_of(y, 3 - l, x), opp)
    x_plus, x_minus = (seq_of(y, l, (x + 1) % 4), ch), (seq_of(y, l, (x + 3) % 4), ch)
    y_plus, y_minus = (seq_of((y + 1) % 4, l, x), ch), (seq_of((y + 3) % 4, l, x), ch)

    bar = pltpu.get_barrier_semaphore()

    @pl.loop(1, 64)
    def _(k):
        pl.semaphore_signal(bar, inc=1, device_id=((s + k) % 64, ch), device_id_type=MESH)

    @pl.loop(1, 4)
    def _(k):
        pl.semaphore_signal(bar, inc=1, device_id=(s, (ch + k) % 4), device_id_type=MESH)

    pl.semaphore_signal(bar, inc=1, device_id=mirror, device_id_type=MESH)

    @pl.loop(0, 32)
    def _(k):
        sender = seq_of(2 * c + k // 16, 2 * (1 - side) + (k // 8) % 2, (k // 2) % 4)
        pl.semaphore_signal(bar, inc=1, device_id=(sender, far + k % 2), device_id_type=MESH)

    loads = [
        pltpu.make_async_copy(tok_in, X, ld.at[0]),
        pltpu.make_async_copy(upf_in, UR, ld.at[1]),
        pltpu.make_async_copy(dnf_in, DR, ld.at[2]),
        pltpu.make_async_copy(left_in, SL, ld.at[3]),
        pltpu.make_async_copy(right_in, SR, ld.at[4]),
        pltpu.make_async_copy(ups_in, US.at[ch, :, pl.ds(0, 96)], ld.at[5]),
        pltpu.make_async_copy(dns_in, DS.at[ch, :, pl.ds(0, 96)], ld.at[6]),
    ]
    for cp in loads:
        cp.start()

    eye = lax.broadcasted_iota(jnp.int32, (128, 128), 0) == lax.broadcasted_iota(jnp.int32, (128, 128), 1)
    loads[0].wait()

    @pl.loop(0, 16)
    def _(k):
        xb = X[k // 2, pl.ds(2 * (k % 2), 2)].reshape(128, W).astype(F32)
        col = jnp.sum(xb * xb, axis=1, keepdims=True)
        SQ[ch, pl.ds(k, 1), :] = jnp.sum(jnp.where(eye, col, 0.0), axis=0, keepdims=True)

    G[ch, 0] = jnp.broadcast_to(gseq_in[...].reshape(1, W), (16, W))
    G[ch, 1] = jnp.broadcast_to(gmlp_in[...].reshape(1, W), (16, W))
    pl.semaphore_wait(bar, 99)

    @pl.loop(1, 4)
    def _(k):
        to = (s, (ch + k) % 4)
        remote(SQ.at[ch], SQ.at[ch], sq_sem.at[0], sq_sem.at[1], to).start()
        remote(G.at[ch], G.at[ch], gm_sem.at[0], gm_sem.at[1], to).start()

    from_lane = lax.broadcasted_iota(jnp.int32, (W, 512), 0)
    to_lane = lax.broadcasted_iota(jnp.int32, (W, 512), 1)
    kept = ((to_lane & 127) < 96) & (from_lane == (to_lane >> 7) * 96 + (to_lane & 127))
    spread = kept.astype(F32).astype(BF16)
    loads[1].wait()
    loads[2].wait()

    @pl.loop(0, 3)
    def _(k):
        at = pl.ds(pl.multiple_of(k * 256, 256), 256)
        UF[ch, at, :] = dot(UR[at, :], spread).astype(BF16)

    @pl.loop(0, 6)
    def _(k):
        at = pl.ds(pl.multiple_of(k * 256, 256), 256)
        DF[ch, at, :] = dot(DR[at, :], spread).astype(BF16)

    ux = y * 4 + x
    uy = x * 4 + y

    def us_unit(blk, u, lanes=pl.ds(0, 1536)):
        return US.at[blk, u // 2, pl.ds(pl.multiple_of((u % 2) * 48, 16), 48), lanes]

    def us_row(blk, r, lanes=pl.ds(0, 1536)):
        return US.at[blk, pl.ds(r * 2, 2), pl.ds(0, 96), lanes]

    def uf_unit(blk, u, lanes=pl.ds(0, 512)):
        return UF.at[blk, pl.ds(pl.multiple_of(u * 48, 16), 48), lanes]

    def uf_row(blk, r, lanes=pl.ds(0, 512)):
        return UF.at[blk, pl.ds(pl.multiple_of(r * 192, 16), 192), lanes]

    def df_unit(blk, u, lanes=pl.ds(0, 512)):
        return DF.at[blk, pl.ds(pl.multiple_of(u * 96, 16), 96), lanes]

    def df_row(blk, r, lanes=pl.ds(0, 512)):
        return DF.at[blk, pl.ds(pl.multiple_of(r * 384, 16), 384), lanes]

    def ds_unit(blk, u, lanes=pl.ds(0, W)):
        return DS.at[blk, u, pl.ds(0, 96), lanes]

    first_unit = [
        remote(ups_in.at[ux // 2, pl.ds(pl.multiple_of((ux % 2) * 48, 16), 48)], us_unit(ch, ux), w1_send.at[0], w1_recv.at[0], mirror),
        remote(uf_unit(ch, uy), uf_unit(ch, uy), w1_send.at[1], w1_recv.at[1], mirror),
        remote(df_unit(ch, uy), df_unit(ch, uy), w1_send.at[2], w1_recv.at[2], mirror),
        remote(dns_in.at[x], ds_unit(ch, x), w1_send.at[3], w1_recv.at[3], mirror),
    ]
    for cp in first_unit:
        cp.start()

    tokens_across = [
        remote(X.at[pl.ds(2 * far, 4), pl.ds(2 * k, 2), 1 - side], XB.at[c], xb_sem.at[0], xb_sem.at[1], (s, far + k))
        for k in range(2)
    ]

    to_sib = (s, sib)
    own_block = [
        remote(ups_in, US.at[ch, :, pl.ds(0, 96)], sib_send.at[0], sib_recv.at[0], to_sib),
        remote(UF.at[ch], UF.at[ch], sib_send.at[1], sib_recv.at[1], to_sib),
        remote(DF.at[ch], DF.at[ch], sib_send.at[2], sib_recv.at[2], to_sib),
        remote(dns_in, DS.at[ch, :, pl.ds(0, 96)], sib_send.at[3], sib_recv.at[3], to_sib),
    ]
    other_block = [
        remote(US.at[opp, :, pl.ds(0, 96)], US.at[opp, :, pl.ds(0, 96)], sib_send.at[4], sib_recv.at[4], to_sib),
        remote(UF.at[opp], UF.at[opp], sib_send.at[5], sib_recv.at[5], to_sib),
        remote(DF.at[opp], DF.at[opp], sib_send.at[6], sib_recv.at[6], to_sib),
        remote(DS.at[opp, :, pl.ds(0, 96)], DS.at[opp, :, pl.ds(0, 96)], sib_send.at[7], sib_recv.at[7], to_sib),
    ]
    for cp in own_block:
        cp.start()

    xring, yring = (x, x_plus, x_minus), (y, y_plus, y_minus)
    ux_of = (lambda p: y * 4 + p, lambda p: p)
    uy_of = (lambda p: x * 4 + p, lambda p: p)
    tables = [
        (us_unit, us_row, 1536, xring, yring, ux_of),
        (uf_unit, uf_row, 512, yring, xring, uy_of),
        (df_unit, df_row, 512, yring, xring, uy_of),
        (ds_unit, None, 384, xring, None, (lambda p: p, None)),
    ]

    def ring_copies(stage, step):
        copies = []
        for j, (unit, row, width, ring_a, ring_b, (first, second)) in enumerate(tables):
            if stage and row is None:
                continue
            pos, plus, minus = (ring_a, ring_b)[stage]
            part, index = ((unit, first), (row, second))[stage]
            sem = ((j * 2 + stage) * 2 + step) * 2
            if step == 0:
                mine = part(opp, index(pos))
                copies += [
                    remote(mine, mine, wr_send.at[sem], wr_recv.at[sem], plus),
                    remote(mine, mine, wr_send.at[sem + 1], wr_recv.at[sem + 1], minus),
                ]
            else:
                half = width // 256 * 128
                below = part(opp, index((pos + 3) % 4), pl.ds(0, half))
                above = part(opp, index((pos + 1) % 4), pl.ds(half, width - half))
                copies += [
                    remote(below, below, wr_send.at[sem], wr_recv.at[sem], plus),
                    remote(above, above, wr_send.at[sem + 1], wr_recv.at[sem + 1], minus),
                ]
        return copies

    rings = [ring_copies(0, 0), ring_copies(0, 1), ring_copies(1, 0), ring_copies(1, 1)]

    US[:, :, pl.ds(96, 32), :] = jnp.zeros((4, 8, 32, 1536), BF16)
    DS[:, :, pl.ds(96, 32), :] = jnp.zeros((4, 4, 32, W), BF16)

    drain(SQ.at[pl.ds(0, 3)], sq_sem.at[1])
    scale = lax.rsqrt((SQ[0] + SQ[1] + SQ[2] + SQ[3]) / 1536.0 + EPS)
    RR[...] = scale
    loads[3].wait()
    gain = gseq_in[...].reshape(1, W).astype(F32)

    @pl.loop(0, 8, unroll=4)
    def _(o):
        r = jnp.concatenate([RR[pl.ds(2 * o, 1), :], RR[pl.ds(2 * o + 1, 1), :]], axis=1)
        lw = (SL[o].astype(F32) * r).astype(BF16)
        FS[o] = (dot(lw, X[o].reshape(256, W)) * gain).astype(BF16)

    out_row = lax.broadcasted_iota(jnp.int32, (256, 256), 0)
    in_row = lax.broadcasted_iota(jnp.int32, (256, 256), 1)
    perm = (in_row == (out_row & 7) * 32 + (out_row >> 5) * 4 + ((out_row >> 3) & 3)).astype(F32).astype(BF16)

    @pl.loop(0, 8)
    def _(k):
        g = (k + s // 8) % 8
        block = FS[:, pl.ds(pl.multiple_of(g * 32, 32), 32), :].reshape(256, W)
        S1[pl.ds(g * 8, 8)] = dot(perm, block).astype(BF16).reshape(8, 32, W)

        @pl.loop(0, 8)
        def _(j):
            d = g * 8 + (j + s) % 8

            @pl.when(d != s)
            def _():
                remote(S1.at[d], R1.at[s], a1_sem.at[0], a1_sem.at[1], (d, ch)).start()

    tokens_across[0].start()
    tokens_across[1].start()
    R1[s] = S1[s]

    @pl.loop(0, 16)
    def _(k):
        col = jnp.sum(jnp.where(eye, RR[pl.ds(k, 1), :], 0.0), axis=1, keepdims=True)
        RC[k // 2, pl.ds(2 * (k % 2), 2)] = jnp.broadcast_to(col, (128, 128)).reshape(2, 2, 32, 128)

    for cp in first_unit:
        cp.wait_recv()
    for cp in rings[0]:
        cp.start()
    for k in range(3):
        for cp in rings[k]:
            cp.wait_recv()
        for cp in rings[k + 1]:
            cp.start()
    loads[4].wait()
    drain(R1.at[pl.ds(0, 63)], a1_sem.at[1])

    @pl.loop(0, 8, unroll=2)
    def _(g):
        part = R1[pl.ds(g * 8, 8)].astype(F32)
        for b in range(4):
            rows = part[:, 8 * b : 8 * b + 8, :].reshape(64, W)
            GB[b, pl.ds(pl.multiple_of(g * 64, 64), 64), :] = rows.astype(BF16)

    low = lax.broadcasted_iota(jnp.int32, (32, 8, W), 1) < 4

    @pl.loop(0, 2)
    def _(k):
        m = (k + y // 2) % 2
        halves = ([], [])
        for pair in range(2):
            even, odd = (
                dot(SR[b, pl.ds(pl.multiple_of(m * 256, 256), 256), :], GB[b]).reshape(32, 8, W)
                for b in (2 * pair, 2 * pair + 1)
            )
            halves[0].append(jnp.where(low, even, pltpu.roll(odd, 4, 1)))
            halves[1].append(jnp.where(low, pltpu.roll(even, 4, 1), odd))
        for half in range(2):
            S2[pl.ds(m * 32, 32), half] = jnp.concatenate(halves[half], axis=1).astype(BF16)

        @pl.loop(0, 32)
        def _(j):
            d = m * 32 + (j + s) % 32
            same = (d // 8) % 2 == side

            @pl.when(same & (d != s))
            def _():
                remote(S2.at[d], R2.at[s], a2_sem.at[0], a2_sem.at[1], (d, ch)).start()

            @pl.when(jnp.logical_not(same))
            def _():
                remote(S2.at[d, h], R2.at[s, h], a2_sem.at[0], a2_sem.at[1], (d, ch)).start()
                remote(
                    S2.at[d, 1 - h], MB.at[c, y % 2, (l % 2) * 4 + x], mb_sem.at[0], mb_sem.at[1], (d, far + y // 2)
                ).start()

    R2[s] = S2[s]
    for cp in rings[3]:
        cp.wait_recv()
    for cp in other_block:
        cp.start()

    out_row = lax.broadcasted_iota(jnp.int32, (128, 128), 0)
    in_row = lax.broadcasted_iota(jnp.int32, (128, 128), 1)
    back = (in_row == ((out_row >> 2) & 7) * 16 + (out_row & 3) * 4 + (out_row >> 5)).astype(F32).astype(BF16)

    def streamed(xs, mixed, rc, gains):
        xs = xs.reshape(128, W).astype(F32)
        rc = rc.reshape(128, 128)
        normed = (xs * jnp.concatenate([rc, rc, rc], axis=1) * gains).astype(BF16).astype(F32)
        return (xs + dot(back, mixed.reshape(128, W)) * normed).astype(BF16).reshape(4, 32, W)

    def at_home(hh, yy, half):
        o4 = pl.ds(4 * hh, 4)
        mixed = R2[pl.ds(yy * 16 + half * 8, 8), hh]
        ST[o4, yy, half] = streamed(X[o4, yy, half], mixed, RC[o4, yy, half], gain)

    drain(R2.at[pl.ds(0, 47)], a2_sem.at[1])

    @pl.loop(0, 4, unroll=2)
    def _(yy):
        at_home(1 - h, yy, side)

    for t in range(2):
        for k in range(2):
            remote(
                ST.at[pl.ds(2 * far + 2 * t, 2), pl.ds(2 * k, 2), side],
                TS.at[ch, pl.ds(2 * t, 2), :, side],
                st_sem.at[0, t], st_sem.at[1, t], (s, far + k),
            ).start()

    @pl.loop(0, 8, unroll=2)
    def _(g):
        at_home(h, g // 2, g % 2)

    for t in range(2):
        remote(
            ST.at[pl.ds(4 * h + 2 * t, 2), pl.ds(2 * (1 - c), 2)], TS.at[ch, pl.ds(2 * t, 2)],
            st_sem.at[0, t], st_sem.at[1, t], to_sib,
        ).start()
    TS[ch] = ST[pl.ds(4 * h, 4), pl.ds(2 * c, 2)]

    drain(G.at[pl.ds(0, 3)], gm_sem.at[1])
    drain(XB, xb_sem.at[1])
    drain(MB, mb_sem.at[1])
    for k in range(2):
        gains = G[far + k, 0, pl.ds(0, 1), :].astype(F32)
        for yy in range(2):
            rc = RC[pl.ds(4 * h, 4), 2 * c + yy, 1 - side]
            TS[far + k, :, yy, 1 - side] = streamed(XB[k, :, yy], MB[k, yy], rc, gains)

    for cp in loads[5:]:
        cp.wait()
    for cp in own_block:
        cp.wait_recv()
    for cp in other_block:
        cp.wait_recv()

    def stream_of(i, at):
        return TS[i, at].reshape(256, W).astype(F32)

    @pl.loop(0, 2)
    def _(t):
        at = pl.ds(2 * t, 2)
        drain(TS.at[0], st_sem.at[1, t])
        squares = jnp.zeros((256, 1), F32)
        for i in range(4):
            v = stream_of(i, at)
            squares += jnp.sum(v * v, axis=1, keepdims=True)
        r2 = lax.rsqrt(squares / 1536.0 + EPS)
        projected = []
        for i in range(4):
            n = (stream_of(i, at) * r2 * G[i, 1, pl.ds(0, 1), :].astype(F32)).astype(BF16)
            projected.append([dot(n, UF[i, pl.ds(g * W, W), :]).astype(BF16) for g in range(2)])
        down = []
        for p in range(4):
            merged = [
                jnp.concatenate([projected[i][g][:, p * 128 : p * 128 + 128] for i in range(4)], axis=1) for g in range(2)
            ]
            acc = jnp.zeros((256, 512), F32)
            for n in range(3):
                lanes = pl.ds(n * 512, 512)
                gate, up = (dot(merged[g], US[p, pl.ds(g * 4, 4), :, lanes].reshape(512, 512)) for g in range(2))
                hidden = (gate / (1.0 + jnp.exp(-gate)) * up).astype(BF16)
                acc += dot(hidden, DF[p, pl.ds(n * 512, 512), :])
            down.append(acc.astype(BF16))
        for r in range(4):
            merged = jnp.concatenate([down[p][:, r * 128 : r * 128 + 128] for p in range(4)], axis=1)
            mlp = dot(merged, DS[r].reshape(512, W))
            OB[r, at] = (stream_of(r, at) + mlp).astype(BF16).reshape(2, 2, 2, 32, W)
        home = (pl.ds(4 * h + 2 * t, 2), pl.ds(2 * c, 2))
        for r in (far, far + 1, sib):
            remote(OB.at[r, at], out.at[home], out_send.at[t], out_recv.at[t], (s, r)).start()
        out[home] = OB[ch, at]

    drain(SQ.at[pl.ds(0, 3)], sq_sem.at[0])
    drain(G.at[pl.ds(0, 3)], gm_sem.at[0])
    drain(XB, xb_sem.at[0])
    drain(S1.at[pl.ds(0, 63)], a1_sem.at[0])
    drain(S2.at[pl.ds(0, 47)], a2_sem.at[0])
    drain(MB, mb_sem.at[0])
    for cp in first_unit + own_block + other_block + rings[0] + rings[1] + rings[2] + rings[3]:
        cp.wait_send()
    for t in range(2):
        drain(TS.at[0], st_sem.at[0, t])
        drain(out.at[pl.ds(0, 3)], out_send.at[t])
        drain(out.at[pl.ds(0, 3)], out_recv.at[t])


def on_device(
    tokens, norm_gain_seq, seq_left, seq_right, norm_gain_mlp, up_first, up_second, down_first, down_second
):
    rows = tokens.shape[0]
    hbm = pl.BlockSpec(memory_space=pl.ANY)
    vmem = pl.BlockSpec(memory_space=pltpu.VMEM)
    dma = pltpu.SemaphoreType.DMA
    out = pl.pallas_call(
        layer_kernel,
        out_shape=jax.ShapeDtypeStruct((8, 4, 2, 32, W), BF16),
        in_specs=[hbm, vmem, vmem] + [hbm] * 6,
        out_specs=pl.BlockSpec(memory_space=pltpu.VMEM),
        scratch_shapes=[
            pltpu.VMEM((8, 4, 2, 32, W), BF16),
            pltpu.VMEM((4, 2, 16, W), BF16),
            pltpu.VMEM((8, 256, 256), BF16),
            pltpu.VMEM((4, 512, 512), BF16),
            pltpu.VMEM((4, 16, 128), F32),
            pltpu.VMEM((16, 128), F32),
            pltpu.VMEM((8, 4, 2, 32, 128), F32),
            pltpu.VMEM((8, 256, W), BF16),
            pltpu.VMEM((64, 32, W), BF16),
            pltpu.VMEM((64, 32, W), BF16),
            pltpu.VMEM((4, 512, W), BF16),
            pltpu.VMEM((64, 2, 16, W), BF16),
            pltpu.VMEM((64, 2, 16, W), BF16),
            pltpu.VMEM((2, 2, 8, 16, W), BF16),
            pltpu.VMEM((2, 4, 2, 32, W), BF16),
            pltpu.VMEM((8, 4, 2, 32, W), BF16),
            pltpu.VMEM((4, 4, 2, 2, 32, W), BF16),
            pltpu.VMEM((4, 4, 2, 2, 32, W), BF16),
            pltpu.VMEM((4, 768, 512), BF16),
            pltpu.VMEM((4, 8, 128, 1536), BF16),
            pltpu.VMEM((4, 1536, 512), BF16),
            pltpu.VMEM((4, 4, 128, W), BF16),
            pltpu.VMEM((768, W), BF16),
            pltpu.VMEM((1536, W), BF16),
            dma((7,)), dma((2,)), dma((2,)), dma((2,)), dma((2,)), dma((2,)), dma((2,)), dma((2, 2)), dma((2,)), dma((2,)),
            dma((4,)), dma((4,)), dma((32,)), dma((32,)), dma((8,)), dma((8,)),
        ],
        compiler_params=pltpu.CompilerParams(
            collective_id=0, has_side_effects=True, vmem_limit_bytes=60 * 2**20
        ),
        name="layer",
    )(
        tokens.reshape(8, 4, 2, 32, W), norm_gain_seq, norm_gain_mlp, seq_left, seq_right, up_first.reshape(768, W),
        up_second.reshape(8, 96, 1536), down_first.reshape(1536, W), down_second.reshape(4, 96, W),
    )
    return out.reshape(rows, 1, W)


def solution(mesh):
    return jax.shard_map(
        on_device,
        mesh=mesh,
        in_specs=(
            P("seq", None, "chan"),
            P("chan"),
            P("seq", None, None),
            P("seq", None, None),
            P("chan"),
            P(None, "chan", None, None),
            P(None, "chan", None, None),
            P("chan", None, None),
            P("chan", None, None),
        ),
        out_specs=P("seq", None, "chan"),
        check_vma=False,
    )
```

time: 182 us -> 163 us (0.90)
  the two profiles are of different devices: /device:TPU:39 before, /device:TPU:71 now
where the time goes in v2:
time: 163 us; the launch traced here: 162 us
  Pallas kernels  160 us (98%)
  local copies, waits for them, and re-layouts  2.71 us (2%)
    pallas_call x1, Pallas kernels, on_device(): pl.pallas_call(layer_kernel, out_shape=jax.ShapeDtypeStruct((8, 4, 2, 32,...  160 us

profile of v2, /device:TPU:71, one launch (start us, length us, event | category | flops | bytes accessed | tf_op | source)
XLA Modules:
  0.0 162.5 jit_solution(15513713824623593608)
XLA Ops:
  0.0 159.8 %layer.1 = bf16[8,4,2,32,384]{4,3,2,1,0:T(8,128)(2,1)} custom-call(bf16[8,4,2,32,384]{4,3,2,1,0:T(8,128)(2,1)} %bitcast.8, bf16[384]{0:T(512)(128)(2,1)} %gseq_in.1, bf16[384]{0:T(512)(128)(2,1)} %gmlp_in.1, bf16[8,256,256]{2,1,0:T(8,128)(2,1)} %left_in.1, bf16[4,512,512]{2,1,0:T(8,128)(2,1)} %right_in.1, bf16[768,384]{1,0:T(8,128)(2,1)} %bitcast.10, ...), custom_call_target="tpu_custom_call" | custom-call | tf_op jit(solution)/shard_map/layer/pallas_call | solution.py:419
  159.8 2.7 %copy.11 = bf16[2048,1,384]{2,0,1:T(8,128)(2,1)} copy(bf16[2048,1,384]{2,0,1:T(8,128)(2,1)} %bitcast.6) | data formatting | bytes 3145728

commit v3 on v2

--- a/solution.py
+++ b/solution.py
@@ -10,6 +10,7 @@
 F32 = jnp.float32
 W = 384
 EPS = 1e-6
+PARTS = ((0, 256), (256, 128))
 
 
 def dot(a, b):
@@ -29,9 +30,11 @@
 def layer_kernel(
     tok_in, gseq_in, gmlp_in, left_in, right_in, upf_in, ups_in, dnf_in, dns_in,
     out,
-    X, G, SL, SR, SQ, RR, RC, FS, S1, R1, GB, S2, R2, MB, XB, ST, TS, OB, UF, US, DF, DS, UR, DR,
-    ld, sq_sem, gm_sem, xb_sem, a1_sem, a2_sem, mb_sem, st_sem, out_send, out_recv, w1_send, w1_recv, wr_send, wr_recv, sib_send, sib_recv,
+    X, G, SL, SR, SQ, RR, RC, FS0, FS1, S10, S11, R10, R11, GB0, GB1, S20, S21, R20, R21, MB0, MB1, XB, ST, TS, OB, UF, US, DF, DS, UR, DR,
+    ld, sq_sem, gm_sem, xb_sem, a1_sem, a2_sem, mb_sem, st_sem, own_sem, out_send, out_recv, w1_send, w1_recv, wr_send, wr_recv, sib_send, sib_recv,
 ):
+    FS, S1, R1, GB = (FS0, FS1), (S10, S11), (R10, R11), (GB0, GB1)
+    S2, R2, MB = (S20, S21), (R20, R21), (MB0, MB1)
     s = lax.axis_index("seq")
     ch = lax.axis_index("chan")
     y, l, x = s // 16, (s // 4) % 4, s % 4
@@ -50,20 +53,15 @@
 
     bar = pltpu.get_barrier_semaphore()
 
-    @pl.loop(1, 64)
+    @pl.loop(1, 64, unroll=9)
     def _(k):
         pl.semaphore_signal(bar, inc=1, device_id=((s + k) % 64, ch), device_id_type=MESH)
 
-    @pl.loop(1, 4)
+    @pl.loop(1, 4, unroll=3)
     def _(k):
         pl.semaphore_signal(bar, inc=1, device_id=(s, (ch + k) % 4), device_id_type=MESH)
 
     pl.semaphore_signal(bar, inc=1, device_id=mirror, device_id_type=MESH)
-
-    @pl.loop(0, 32)
-    def _(k):
-        sender = seq_of(2 * c + k // 16, 2 * (1 - side) + (k // 8) % 2, (k // 2) % 4)
-        pl.semaphore_signal(bar, inc=1, device_id=(sender, far + k % 2), device_id_type=MESH)
 
     loads = [
         pltpu.make_async_copy(tok_in, X, ld.at[0]),
@@ -88,7 +86,7 @@
 
     G[ch, 0] = jnp.broadcast_to(gseq_in[...].reshape(1, W), (16, W))
     G[ch, 1] = jnp.broadcast_to(gmlp_in[...].reshape(1, W), (16, W))
-    pl.semaphore_wait(bar, 99)
+    pl.semaphore_wait(bar, 67)
 
     @pl.loop(1, 4)
     def _(k):
@@ -212,33 +210,43 @@
     loads[3].wait()
     gain = gseq_in[...].reshape(1, W).astype(F32)
 
-    @pl.loop(0, 8, unroll=4)
-    def _(o):
-        r = jnp.concatenate([RR[pl.ds(2 * o, 1), :], RR[pl.ds(2 * o + 1, 1), :]], axis=1)
-        lw = (SL[o].astype(F32) * r).astype(BF16)
-        FS[o] = (dot(lw, X[o].reshape(256, W)) * gain).astype(BF16)
-
     out_row = lax.broadcasted_iota(jnp.int32, (256, 256), 0)
     in_row = lax.broadcasted_iota(jnp.int32, (256, 256), 1)
     perm = (in_row == (out_row & 7) * 32 + (out_row >> 5) * 4 + ((out_row >> 3) & 3)).astype(F32).astype(BF16)
 
-    @pl.loop(0, 8)
-    def _(k):
-        g = (k + s // 8) % 8
-        block = FS[:, pl.ds(pl.multiple_of(g * 32, 32), 32), :].reshape(256, W)
-        S1[pl.ds(g * 8, 8)] = dot(perm, block).astype(BF16).reshape(8, 32, W)
+    def first(n):
+        start, width = PARTS[n]
+        cut = pl.ds(start, width)
+        fs, s1, r1 = FS[n], S1[n], R1[n]
+
+        @pl.loop(0, 8, unroll=4)
+        def _(o):
+            if n == 0:
+                r = jnp.concatenate([RR[pl.ds(2 * o, 1), :], RR[pl.ds(2 * o + 1, 1), :]], axis=1)
+                SL[o] = (SL[o].astype(F32) * r).astype(BF16)
+            rows = X[o, :, :, :, cut].reshape(256, width)
+            fs[o] = (dot(SL[o], rows) * gain[:, start : start + width]).astype(BF16)
 
         @pl.loop(0, 8)
-        def _(j):
-            d = g * 8 + (j + s) % 8
-
-            @pl.when(d != s)
-            def _():
-                remote(S1.at[d], R1.at[s], a1_sem.at[0], a1_sem.at[1], (d, ch)).start()
-
+        def _(k):
+            g = (k + s // 8) % 8
+            block = fs[:, pl.ds(pl.multiple_of(g * 32, 32), 32), :].reshape(256, width)
+            s1[pl.ds(g * 8, 8)] = dot(perm, block).astype(BF16).reshape(8, 32, width)
+
+            @pl.loop(0, 8, unroll=8)
+            def _(j):
+                d = g * 8 + (j + s) % 8
+
+                @pl.when(d != s)
+                def _():
+                    remote(s1.at[d], r1.at[s], a1_sem.at[0, n], a1_sem.at[1, n], (d, ch)).start()
+
+        r1[s] = s1[s]
+
+    first(0)
+    first(1)
     tokens_across[0].start()
     tokens_across[1].start()
-    R1[s] = S1[s]
 
     @pl.loop(0, 16)
     def _(k):
@@ -255,48 +263,56 @@
         for cp in rings[k + 1]:
             cp.start()
     loads[4].wait()
-    drain(R1.at[pl.ds(0, 63)], a1_sem.at[1])
-
-    @pl.loop(0, 8, unroll=2)
-    def _(g):
-        part = R1[pl.ds(g * 8, 8)].astype(F32)
-        for b in range(4):
-            rows = part[:, 8 * b : 8 * b + 8, :].reshape(64, W)
-            GB[b, pl.ds(pl.multiple_of(g * 64, 64), 64), :] = rows.astype(BF16)
-
-    low = lax.broadcasted_iota(jnp.int32, (32, 8, W), 1) < 4
-
-    @pl.loop(0, 2)
-    def _(k):
-        m = (k + y // 2) % 2
-        halves = ([], [])
-        for pair in range(2):
-            even, odd = (
-                dot(SR[b, pl.ds(pl.multiple_of(m * 256, 256), 256), :], GB[b]).reshape(32, 8, W)
-                for b in (2 * pair, 2 * pair + 1)
-            )
-            halves[0].append(jnp.where(low, even, pltpu.roll(odd, 4, 1)))
-            halves[1].append(jnp.where(low, pltpu.roll(even, 4, 1), odd))
-        for half in range(2):
-            S2[pl.ds(m * 32, 32), half] = jnp.concatenate(halves[half], axis=1).astype(BF16)
-
-        @pl.loop(0, 32)
-        def _(j):
-            d = m * 32 + (j + s) % 32
-            same = (d // 8) % 2 == side
-
-            @pl.when(same & (d != s))
-            def _():
-                remote(S2.at[d], R2.at[s], a2_sem.at[0], a2_sem.at[1], (d, ch)).start()
-
-            @pl.when(jnp.logical_not(same))
-            def _():
-                remote(S2.at[d, h], R2.at[s, h], a2_sem.at[0], a2_sem.at[1], (d, ch)).start()
-                remote(
-                    S2.at[d, 1 - h], MB.at[c, y % 2, (l % 2) * 4 + x], mb_sem.at[0], mb_sem.at[1], (d, far + y // 2)
-                ).start()
-
-    R2[s] = S2[s]
+
+    def second(n):
+        width = PARTS[n][1]
+        r1, gb, s2, r2, mb = R1[n], GB[n], S2[n], R2[n], MB[n]
+        drain(r1.at[pl.ds(0, 63)], a1_sem.at[1, n])
+
+        @pl.loop(0, 8, unroll=2)
+        def _(g):
+            part = r1[pl.ds(g * 8, 8)].astype(F32)
+            for b in range(4):
+                rows = part[:, 8 * b : 8 * b + 8, :].reshape(64, width)
+                gb[b, pl.ds(pl.multiple_of(g * 64, 64), 64), :] = rows.astype(BF16)
+
+        low = lax.broadcasted_iota(jnp.int32, (32, 8, width), 1) < 4
+
+        @pl.loop(0, 2)
+        def _(k):
+            m = (k + y // 2) % 2
+            halves = ([], [])
+            for pair in range(2):
+                even, odd = (
+                    dot(SR[b, pl.ds(pl.multiple_of(m * 256, 256), 256), :], gb[b]).reshape(32, 8, width)
+                    for b in (2 * pair, 2 * pair + 1)
+                )
+                halves[0].append(jnp.where(low, even, pltpu.roll(odd, 4, 1)))
+                halves[1].append(jnp.where(low, pltpu.roll(even, 4, 1), odd))
+            for half in range(2):
+                s2[pl.ds(m * 32, 32), half] = jnp.concatenate(halves[half], axis=1).astype(BF16)
+
+            @pl.loop(0, 32, unroll=8)
+            def _(j):
+                d = m * 32 + (j + s) % 32
+                same = (d // 8) % 2 == side
+
+                @pl.when(same & (d != s))
+                def _():
+                    remote(s2.at[d], r2.at[s], a2_sem.at[0, n], a2_sem.at[1, n], (d, ch)).start()
+
+                @pl.when(jnp.logical_not(same))
+                def _():
+                    remote(s2.at[d, h], r2.at[s, h], a2_sem.at[0, n], a2_sem.at[1, n], (d, ch)).start()
+                    remote(
+                        s2.at[d, 1 - h], mb.at[c, y % 2, (l % 2) * 4 + x],
+                        mb_sem.at[0, n], mb_sem.at[1, n], (d, far + y // 2),
+                    ).start()
+
+        r2[s] = s2[s]
+
+    second(0)
+    second(1)
     for cp in rings[3]:
         cp.wait_recv()
     for cp in other_block:
@@ -307,21 +323,35 @@
     back = (in_row == ((out_row >> 2) & 7) * 16 + (out_row & 3) * 4 + (out_row >> 5)).astype(F32).astype(BF16)
 
     def streamed(xs, mixed, rc, gains):
-        xs = xs.reshape(128, W).astype(F32)
-        rc = rc.reshape(128, 128)
-        normed = (xs * jnp.concatenate([rc, rc, rc], axis=1) * gains).astype(BF16).astype(F32)
-        return (xs + dot(back, mixed.reshape(128, W)) * normed).astype(BF16).reshape(4, 32, W)
-
-    def at_home(hh, yy, half):
-        o4 = pl.ds(4 * hh, 4)
-        mixed = R2[pl.ds(yy * 16 + half * 8, 8), hh]
-        ST[o4, yy, half] = streamed(X[o4, yy, half], mixed, RC[o4, yy, half], gain)
-
-    drain(R2.at[pl.ds(0, 47)], a2_sem.at[1])
+        width = xs.shape[-1]
+        xs = xs.reshape(128, width).astype(F32)
+        rc = jnp.concatenate([rc.reshape(128, 128)] * (width // 128), axis=1)
+        normed = (xs * rc * gains).astype(BF16).astype(F32)
+        return (xs + dot(back, mixed.reshape(128, width)) * normed).astype(BF16).reshape(4, 32, width)
+
+    def at_home(n, hh, yy, half):
+        start, width = PARTS[n]
+        o4, cut = pl.ds(4 * hh, 4), pl.ds(start, width)
+        mixed = R2[n][pl.ds(yy * 16 + half * 8, 8), hh]
+        ST[o4, yy, half, :, cut] = streamed(
+            X[o4, yy, half, :, cut], mixed, RC[o4, yy, half], gain[:, start : start + width]
+        )
+
+    drain(R2[0].at[pl.ds(0, 47)], a2_sem.at[1, 0])
 
     @pl.loop(0, 4, unroll=2)
     def _(yy):
-        at_home(1 - h, yy, side)
+        at_home(0, 1 - h, yy, side)
+
+    @pl.loop(0, 8, unroll=2)
+    def _(g):
+        at_home(0, h, g // 2, g % 2)
+
+    drain(R2[1].at[pl.ds(0, 47)], a2_sem.at[1, 1])
+
+    @pl.loop(0, 4, unroll=2)
+    def _(yy):
+        at_home(1, 1 - h, yy, side)
 
     for t in range(2):
         for k in range(2):
@@ -333,7 +363,7 @@
 
     @pl.loop(0, 8, unroll=2)
     def _(g):
-        at_home(h, g // 2, g % 2)
+        at_home(1, h, g // 2, g % 2)
 
     for t in range(2):
         remote(
@@ -344,12 +374,14 @@
 
     drain(G.at[pl.ds(0, 3)], gm_sem.at[1])
     drain(XB, xb_sem.at[1])
-    drain(MB, mb_sem.at[1])
-    for k in range(2):
-        gains = G[far + k, 0, pl.ds(0, 1), :].astype(F32)
-        for yy in range(2):
-            rc = RC[pl.ds(4 * h, 4), 2 * c + yy, 1 - side]
-            TS[far + k, :, yy, 1 - side] = streamed(XB[k, :, yy], MB[k, yy], rc, gains)
+    for n, (start, width) in enumerate(PARTS):
+        cut = pl.ds(start, width)
+        drain(MB[n], mb_sem.at[1, n])
+        for k in range(2):
+            gains = G[far + k, 0, pl.ds(0, 1), cut].astype(F32)
+            for yy in range(2):
+                rc = RC[pl.ds(4 * h, 4), 2 * c + yy, 1 - side]
+                TS[far + k, :, yy, 1 - side, :, cut] = streamed(XB[k, :, yy, :, cut], MB[n][k, yy], rc, gains)
 
     for cp in loads[5:]:
         cp.wait()
@@ -393,20 +425,22 @@
         home = (pl.ds(4 * h + 2 * t, 2), pl.ds(2 * c, 2))
         for r in (far, far + 1, sib):
             remote(OB.at[r, at], out.at[home], out_send.at[t], out_recv.at[t], (s, r)).start()
-        out[home] = OB[ch, at]
+        pltpu.make_async_copy(OB.at[ch, at], out.at[home], own_sem.at[t]).start()
 
     drain(SQ.at[pl.ds(0, 3)], sq_sem.at[0])
     drain(G.at[pl.ds(0, 3)], gm_sem.at[0])
     drain(XB, xb_sem.at[0])
-    drain(S1.at[pl.ds(0, 63)], a1_sem.at[0])
-    drain(S2.at[pl.ds(0, 47)], a2_sem.at[0])
-    drain(MB, mb_sem.at[0])
+    for n in range(2):
+        drain(S1[n].at[pl.ds(0, 63)], a1_sem.at[0, n])
+        drain(S2[n].at[pl.ds(0, 47)], a2_sem.at[0, n])
+        drain(MB[n], mb_sem.at[0, n])
     for cp in first_unit + own_block + other_block + rings[0] + rings[1] + rings[2] + rings[3]:
         cp.wait_send()
     for t in range(2):
         drain(TS.at[0], st_sem.at[0, t])
         drain(out.at[pl.ds(0, 3)], out_send.at[t])
         drain(out.at[pl.ds(0, 3)], out_recv.at[t])
+        drain(out.at[pl.ds(0, 1)], own_sem.at[t])
 
 
 def on_device(
@@ -420,7 +454,7 @@
         layer_kernel,
         out_shape=jax.ShapeDtypeStruct((8, 4, 2, 32, W), BF16),
         in_specs=[hbm, vmem, vmem] + [hbm] * 6,
-        out_specs=pl.BlockSpec(memory_space=pltpu.VMEM),
+        out_specs=hbm,
         scratch_shapes=[
             pltpu.VMEM((8, 4, 2, 32, W), BF16),
             pltpu.VMEM((4, 2, 16, W), BF16),
@@ -429,13 +463,13 @@
             pltpu.VMEM((4, 16, 128), F32),
             pltpu.VMEM((16, 128), F32),
             pltpu.VMEM((8, 4, 2, 32, 128), F32),
-            pltpu.VMEM((8, 256, W), BF16),
-            pltpu.VMEM((64, 32, W), BF16),
-            pltpu.VMEM((64, 32, W), BF16),
-            pltpu.VMEM((4, 512, W), BF16),
-            pltpu.VMEM((64, 2, 16, W), BF16),
-            pltpu.VMEM((64, 2, 16, W), BF16),
-            pltpu.VMEM((2, 2, 8, 16, W), BF16),
+            *[pltpu.VMEM((8, 256, w), BF16) for _, w in PARTS],
+            *[pltpu.VMEM((64, 32, w), BF16) for _, w in PARTS],
+            *[pltpu.VMEM((64, 32, w), BF16) for _, w in PARTS],
+            *[pltpu.VMEM((4, 512, w), BF16) for _, w in PARTS],
+            *[pltpu.VMEM((64, 2, 16, w), BF16) for _, w in PARTS],
+            *[pltpu.VMEM((64, 2, 16, w), BF16) for _, w in PARTS],
+            *[pltpu.VMEM((2, 2, 8, 16, w), BF16) for _, w in PARTS],
             pltpu.VMEM((2, 4, 2, 32, W), BF16),
             pltpu.VMEM((8, 4, 2, 32, W), BF16),
             pltpu.VMEM((4, 4, 2, 2, 32, W), BF16),
@@ -446,7 +480,7 @@
             pltpu.VMEM((4, 4, 128, W), BF16),
             pltpu.VMEM((768, W), BF16),
             pltpu.VMEM((1536, W), BF16),
-            dma((7,)), dma((2,)), dma((2,)), dma((2,)), dma((2,)), dma((2,)), dma((2,)), dma((2, 2)), dma((2,)), dma((2,)),
+            dma((7,)), dma((2,)), dma((2,)), dma((2,)), dma((2, 2)), dma((2, 2)), dma((2, 2)), dma((2, 2)), dma((2,)), dma((2,)), dma((2,)),
             dma((4,)), dma((4,)), dma((32,)), dma((32,)), dma((8,)), dma((8,)),
         ],
         compiler_params=pltpu.CompilerParams(

time: 163 us -> 158 us (0.969)
  the two profiles are of different devices: /device:TPU:71 before, /device:TPU:1 now
where the time goes in v3:
time: 158 us
  Pallas kernels  155 us (98%)
  local copies, waits for them, and re-layouts  2.71 us (2%)
    pallas_call x1, Pallas kernels, on_device(): pl.pallas_call(layer_kernel, out_shape=jax.ShapeDtypeStruct((8, 4, 2, 32,...  155 us

profile of v3, /device:TPU:1, one launch (start us, length us, event | category | flops | bytes accessed | tf_op | source)
XLA Modules:
  0.0 158.0 jit_solution(615070378019262683)
XLA Ops:
  0.0 155.3 %layer.1 = bf16[8,4,2,32,384]{4,3,2,1,0:T(8,128)(2,1)} custom-call(bf16[8,4,2,32,384]{4,3,2,1,0:T(8,128)(2,1)} %bitcast.8, bf16[384]{0:T(512)(128)(2,1)} %gseq_in.1, bf16[384]{0:T(512)(128)(2,1)} %gmlp_in.1, bf16[8,256,256]{2,1,0:T(8,128)(2,1)} %left_in.1, bf16[4,512,512]{2,1,0:T(8,128)(2,1)} %right_in.1, bf16[768,384]{1,0:T(8,128)(2,1)} %bitcast.10, ...), custom_call_target="tpu_custom_call" | custom-call | tf_op jit(solution)/shard_map/layer/pallas_call | solution.py:453
  155.3 2.7 %copy.11 = bf16[2048,1,384]{2,0,1:T(8,128)(2,1)} copy(bf16[2048,1,384]{2,0,1:T(8,128)(2,1)} %bitcast.6) | data formatting | bytes 3145728

commit v4 on v3

--- a/solution.py
+++ b/solution.py
@@ -31,7 +31,7 @@
     tok_in, gseq_in, gmlp_in, left_in, right_in, upf_in, ups_in, dnf_in, dns_in,
     out,
     X, G, SL, SR, SQ, RR, RC, FS0, FS1, S10, S11, R10, R11, GB0, GB1, S20, S21, R20, R21, MB0, MB1, XB, ST, TS, OB, UF, US, DF, DS, UR, DR,
-    ld, sq_sem, gm_sem, xb_sem, a1_sem, a2_sem, mb_sem, st_sem, own_sem, out_send, out_recv, w1_send, w1_recv, wr_send, wr_recv, sib_send, sib_recv,
+    met, ld, sq_sem, gm_sem, xb_sem, a1_sem, a2_sem, mb_sem, st_sem, own_sem, out_send, out_recv, w1_send, w1_recv, wr_send, wr_recv, sib_send, sib_recv,
 ):
     FS, S1, R1, GB = (FS0, FS1), (S10, S11), (R10, R11), (GB0, GB1)
     S2, R2, MB = (S20, S21), (R20, R21), (MB0, MB1)
@@ -53,9 +53,15 @@
 
     bar = pltpu.get_barrier_semaphore()
 
-    @pl.loop(1, 64, unroll=9)
-    def _(k):
-        pl.semaphore_signal(bar, inc=1, device_id=((s + k) % 64, ch), device_id_type=MESH)
+    x_line = [(seq_of(y, l, (x + k) % 4), ch) for k in (1, 2, 3)]
+    y_line = [(seq_of((y + k) % 4, l, x), ch) for k in (1, 2, 3)]
+    z_line = [(seq_of(y, (l + k) % 4, x), ch) for k in (1, 2, 3)]
+
+    def greet(sem, line):
+        for to in line:
+            pl.semaphore_signal(sem, inc=1, device_id=to, device_id_type=MESH)
+
+    greet(bar, x_line + y_line + z_line)
 
     @pl.loop(1, 4, unroll=3)
     def _(k):
@@ -86,13 +92,15 @@
 
     G[ch, 0] = jnp.broadcast_to(gseq_in[...].reshape(1, W), (16, W))
     G[ch, 1] = jnp.broadcast_to(gmlp_in[...].reshape(1, W), (16, W))
-    pl.semaphore_wait(bar, 67)
+    pl.semaphore_wait(bar, 13)
 
     @pl.loop(1, 4)
     def _(k):
         to = (s, (ch + k) % 4)
         remote(SQ.at[ch], SQ.at[ch], sq_sem.at[0], sq_sem.at[1], to).start()
         remote(G.at[ch], G.at[ch], gm_sem.at[0], gm_sem.at[1], to).start()
+
+    greet(met.at[0], y_line)
 
     from_lane = lax.broadcasted_iota(jnp.int32, (W, 512), 0)
     to_lane = lax.broadcasted_iota(jnp.int32, (W, 512), 1)
@@ -110,6 +118,9 @@
     def _(k):
         at = pl.ds(pl.multiple_of(k * 256, 256), 256)
         DF[ch, at, :] = dot(DR[at, :], spread).astype(BF16)
+
+    pl.semaphore_wait(met.at[0], 3)
+    greet(met.at[1], z_line)
 
     ux = y * 4 + x
     uy = x * 4 + y
@@ -243,6 +254,7 @@
 
         r1[s] = s1[s]
 
+    pl.semaphore_wait(met.at[1], 3)
     first(0)
     first(1)
     tokens_across[0].start()
@@ -257,11 +269,10 @@
         cp.wait_recv()
     for cp in rings[0]:
         cp.start()
-    for k in range(3):
-        for cp in rings[k]:
-            cp.wait_recv()
-        for cp in rings[k + 1]:
-            cp.start()
+    for cp in rings[0]:
+        cp.wait_recv()
+    for cp in rings[1]:
+        cp.start()
     loads[4].wait()
 
     def second(n):
@@ -312,10 +323,14 @@
         r2[s] = s2[s]
 
     second(0)
+    for cp in rings[1]:
+        cp.wait_recv()
+    for cp in rings[2]:
+        cp.start()
     second(1)
+    for cp in rings[2]:
+        cp.wait_recv()
     for cp in rings[3]:
-        cp.wait_recv()
-    for cp in other_block:
         cp.start()
 
     out_row = lax.broadcasted_iota(jnp.int32, (128, 128), 0)
@@ -347,6 +362,10 @@
     def _(g):
         at_home(0, h, g // 2, g % 2)
 
+    for cp in rings[3]:
+        cp.wait_recv()
+    for cp in other_block:
+        cp.start()
     drain(R2[1].at[pl.ds(0, 47)], a2_sem.at[1, 1])
 
     @pl.loop(0, 4, unroll=2)
@@ -480,6 +499,7 @@
             pltpu.VMEM((4, 4, 128, W), BF16),
             pltpu.VMEM((768, W), BF16),
             pltpu.VMEM((1536, W), BF16),
+            pltpu.SemaphoreType.REGULAR((2,)),
             dma((7,)), dma((2,)), dma((2,)), dma((2,)), dma((2, 2)), dma((2, 2)), dma((2, 2)), dma((2, 2)), dma((2,)), dma((2,)), dma((2,)),
             dma((4,)), dma((4,)), dma((32,)), dma((32,)), dma((8,)), dma((8,)),
         ],

time: 158 us -> 154 us (0.975)
  the two profiles are of different devices: /device:TPU:1 before, /device:TPU:71 now
where the time goes in v4:
time: 154 us; the launch traced here: 153 us
  Pallas kernels  150 us (97%)
  local copies, waits for them, and re-layouts  2.71 us (2%)
    pallas_call x1, Pallas kernels, on_device(): pl.pallas_call(layer_kernel, out_shape=jax.ShapeDtypeStruct((8, 4, 2, 32,...  150 us

profile of v4, /device:TPU:71, one launch (start us, length us, event | category | flops | bytes accessed | tf_op | source)
XLA Modules:
  0.0 152.7 jit_solution(5474953669804682494)
XLA Ops:
  0.0 150.0 %layer.1 = bf16[8,4,2,32,384]{4,3,2,1,0:T(8,128)(2,1)} custom-call(bf16[8,4,2,32,384]{4,3,2,1,0:T(8,128)(2,1)} %bitcast.8, bf16[384]{0:T(512)(128)(2,1)} %gseq_in.1, bf16[384]{0:T(512)(128)(2,1)} %gmlp_in.1, bf16[8,256,256]{2,1,0:T(8,128)(2,1)} %left_in.1, bf16[4,512,512]{2,1,0:T(8,128)(2,1)} %right_in.1, bf16[768,384]{1,0:T(8,128)(2,1)} %bitcast.10, ...), custom_call_target="tpu_custom_call" | custom-call | tf_op jit(solution)/shard_map/layer/pallas_call | solution.py:472
  150.0 2.7 %copy.11 = bf16[2048,1,384]{2,0,1:T(8,128)(2,1)} copy(bf16[2048,1,384]{2,0,1:T(8,128)(2,1)} %bitcast.6) | data formatting | bytes 3145728

commit v5 on v4

--- a/solution.py
+++ b/solution.py
@@ -410,13 +410,18 @@
         cp.wait_recv()
 
     def stream_of(i, at):
-        return TS[i, at].reshape(256, W).astype(F32)
-
-    @pl.loop(0, 2)
-    def _(t):
-        at = pl.ds(2 * t, 2)
-        drain(TS.at[0], st_sem.at[1, t])
-        squares = jnp.zeros((256, 1), F32)
+        return TS[i, at].reshape(128, W).astype(F32)
+
+    @pl.loop(0, 4)
+    def _(o):
+        t = o // 2
+        at = pl.ds(o, 1)
+
+        @pl.when(o % 2 == 0)
+        def _():
+            drain(TS.at[0], st_sem.at[1, t])
+
+        squares = jnp.zeros((128, 1), F32)
         for i in range(4):
             v = stream_of(i, at)
             squares += jnp.sum(v * v, axis=1, keepdims=True)
@@ -430,7 +435,7 @@
             merged = [
                 jnp.concatenate([projected[i][g][:, p * 128 : p * 128 + 128] for i in range(4)], axis=1) for g in range(2)
             ]
-            acc = jnp.zeros((256, 512), F32)
+            acc = jnp.zeros((128, 512), F32)
             for n in range(3):
                 lanes = pl.ds(n * 512, 512)
                 gate, up = (dot(merged[g], US[p, pl.ds(g * 4, 4), :, lanes].reshape(512, 512)) for g in range(2))
@@ -440,8 +445,8 @@
         for r in range(4):
             merged = jnp.concatenate([down[p][:, r * 128 : r * 128 + 128] for p in range(4)], axis=1)
             mlp = dot(merged, DS[r].reshape(512, W))
-            OB[r, at] = (stream_of(r, at) + mlp).astype(BF16).reshape(2, 2, 2, 32, W)
-        home = (pl.ds(4 * h + 2 * t, 2), pl.ds(2 * c, 2))
+            OB[r, at] = (stream_of(r, at) + mlp).astype(BF16).reshape(1, 2, 2, 32, W)
+        home = (pl.ds(4 * h + o, 1), pl.ds(2 * c, 2))
         for r in (far, far + 1, sib):
             remote(OB.at[r, at], out.at[home], out_send.at[t], out_recv.at[t], (s, r)).start()
         pltpu.make_async_copy(OB.at[ch, at], out.at[home], own_sem.at[t]).start()

time: 154 us -> 153 us (level)
  Pallas kernels: 150 us -> 148 us
    pallas_call x1, Pallas kernels: 150 us -> 148 us  [on_device(): pl.pallas_call(layer_kernel, out_shape=jax.ShapeDtypeStruct((8, 4, 2, 32,...]
where the time goes in v5:
time: 153 us; the launch traced here: 150 us
  Pallas kernels  148 us (97%)
  local copies, waits for them, and re-layouts  2.71 us (2%)
    pallas_call x1, Pallas kernels, on_device(): pl.pallas_call(layer_kernel, out_shape=jax.ShapeDtypeStruct((8, 4, 2, 32,...  148 us

profile of v5, /device:TPU:71, one launch (start us, length us, event | category | flops | bytes accessed | tf_op | source)
XLA Modules:
  0.0 150.4 jit_solution(2656819101510931699)
XLA Ops:
  0.0 147.7 %layer.1 = bf16[8,4,2,32,384]{4,3,2,1,0:T(8,128)(2,1)} custom-call(bf16[8,4,2,32,384]{4,3,2,1,0:T(8,128)(2,1)} %bitcast.8, bf16[384]{0:T(512)(128)(2,1)} %gseq_in.1, bf16[384]{0:T(512)(128)(2,1)} %gmlp_in.1, bf16[8,256,256]{2,1,0:T(8,128)(2,1)} %left_in.1, bf16[4,512,512]{2,1,0:T(8,128)(2,1)} %right_in.1, bf16[768,384]{1,0:T(8,128)(2,1)} %bitcast.10, ...), custom_call_target="tpu_custom_call" | custom-call | tf_op jit(solution)/shard_map/layer/pallas_call | solution.py:477
  147.7 2.7 %copy.11 = bf16[2048,1,384]{2,0,1:T(8,128)(2,1)} copy(bf16[2048,1,384]{2,0,1:T(8,128)(2,1)} %bitcast.6) | data formatting | bytes 3145728
